TPU v7x, 32 devices: a whole 2x2x4 slice. The times are simulated.
32 devices in a mesh: dp: 4 (over y, x), mp: 8 (over z, core).
Axes of the slice: x: 2, y: 2, z: 4, core: 2. Of those that a mesh axis runs over, the one named last changes fastest.
Arguments:
- grads_a: bfloat16 [4, 4, 1792, 576], P('dp', None, 'mp'), may hold values from -360 to 360
- momentum_a: float32 [7168, 576], P(('dp', 'mp')), may hold values from -6 to 6
- weights_a: bfloat16 [7168, 576], P(('dp', 'mp')), may hold values from -6 to 6
- up_gradient_parts: bfloat16 [4, 4, 4096, 512], P('dp', None, 'mp'), may hold values from -360 to 360
- up_momentum_buffer: float32 [16384, 512], P(('dp', 'mp')), may hold values from -6 to 6
- up_weight_before: bfloat16 [16384, 512], P(('dp', 'mp')), may hold values from -6 to 6
Outputs:
- new_weight_a: bfloat16 [4, 1792, 576], P(None, 'mp')
- new_momentum_a: float32 [7168, 576], P(('dp', 'mp'))
- update_a: float32 [7168, 576], P(('dp', 'mp'))
- new_weight_b: bfloat16 [4, 4096, 512], P(None, 'mp')
- new_momentum_b: float32 [16384, 512], P(('dp', 'mp'))
- up_scaled_update: float32 [16384, 512], P(('dp', 'mp'))
All inputs are finite; a program needn't handle non-finite values.
Results may differ from a plain program's by a relative error of at most 0.008.
Values may be sent and summed in bfloat16 or wider, within the bound.
A program may use at most 64 MiB of HBM per device.

v0:
```python
import math

import jax
import jax.numpy as jnp
from jax import lax
from jax.sharding import PartitionSpec as P

D = 7168
KEY_VALUE_ROWS = 16384
ITERS = 3


COEF_A = 3.4445
COEF_B = -4.775
COEF_C = 2.0315
MOMENT = 0.95
RATE = 0.2
DECAY = 0.1
EPSILON = 1e-07
PRECISE = lax.Precision.HIGHEST


def gram_of(value):
    return jnp.dot(value.T, value, precision=PRECISE, preferred_element_type=jnp.float32)


def newton(iterate, gram_matrix):
    squared = jnp.dot(
        gram_matrix, gram_matrix, precision=PRECISE, preferred_element_type=jnp.float32
    )
    polynomial = COEF_B * gram_matrix + COEF_C * squared
    return COEF_A * iterate + jnp.dot(
        iterate, polynomial, precision=PRECISE, preferred_element_type=jnp.float32
    )


def local(grads_a, momentum_a, weights_a, up_gradient_parts, up_momentum_buffer, up_weight_before):
    sum_a, sum_b = (
        lax.psum_scatter(
            grads_a[0].astype(jnp.float32).astype(jnp.bfloat16),
            "dp",
            scatter_dimension=0,
            tiled=True,
        ).astype(jnp.float32),
        lax.psum_scatter(
            up_gradient_parts[0].astype(jnp.float32).astype(jnp.bfloat16),
            "dp",
            scatter_dimension=0,
            tiled=True,
        ).astype(jnp.float32),
    )
    summed = [sum_a[0], sum_b[0]]
    states = [momentum_a, up_momentum_buffer]
    olds = [weights_a.astype(jnp.float32), up_weight_before.astype(jnp.float32)]
    new_states = [MOMENT * states[0] + summed[0], MOMENT * states[1] + summed[1]]
    directions = [summed[0] + MOMENT * new_states[0], summed[1] + MOMENT * new_states[1]]
    square_a, square_b = lax.psum(
        (jnp.sum(directions[0] * directions[0]), jnp.sum(directions[1] * directions[1])),
        ("dp", "mp"),
    )
    iterates = [
        directions[0] / (jnp.sqrt(square_a) + EPSILON),
        directions[1] / (jnp.sqrt(square_b) + EPSILON),
    ]
    for step in range(ITERS):
        gram_a, gram_b = lax.psum((gram_of(iterates[0]), gram_of(iterates[1])), ("dp", "mp"))
        iterates = [newton(iterates[0], gram_a), newton(iterates[1], gram_b)]
    updates = [0.2 * math.sqrt(D) * iterates[0], 0.2 * math.sqrt(KEY_VALUE_ROWS) * iterates[1]]
    new_rows = [
        (olds[0] * (1.0 - RATE * DECAY) - RATE * updates[0]).astype(jnp.bfloat16),
        (olds[1] * (1.0 - RATE * DECAY) - RATE * updates[1]).astype(jnp.bfloat16),
    ]
    weight_a, up_weight_matrix = (
        lax.all_gather(new_rows[0][None], "dp", axis=0, tiled=True),
        lax.all_gather(new_rows[1][None], "dp", axis=0, tiled=True),
    )
    return (weight_a, new_states[0], updates[0], up_weight_matrix, new_states[1], updates[1])


def solution(mesh):
    placed = (
        P("dp", None, "mp", None),
        P(("dp", "mp"), None),
        P(("dp", "mp"), None),
        P("dp", None, "mp", None),
        P(("dp", "mp"), None),
        P(("dp", "mp"), None),
    )
    return jax.shard_map(
        local,
        mesh=mesh,
        in_specs=placed,
        out_specs=(
            P(None, "mp", None),
            P(("dp", "mp"), None),
            P(("dp", "mp"), None),
            P(None, "mp", None),
            P(("dp", "mp"), None),
            P(("dp", "mp"), None),
        ),
        check_vma=False,
    )
```

profile of v0, /device:TPU:1, one launch (start us, length us, event | category | flops | bytes accessed | tf_op | source)
XLA Modules:
  0.0 627.4 jit_solution(17877398632010433399)
XLA Ops:
  7.2 0.0 reduce-scatter.7.cloned.1.call-start
  7.2 0.0 copy-start.8
  7.2 0.7 reduce-scatter.7.cloned.1.call-update
  7.9 0.0 reduce-scatter.9.cloned.1.call-start
  7.9 0.0 copy-start.6
  8.0 0.7 reduce-scatter.9.cloned.1.call-update
  8.6 0.0 all-reduce.14.cloned.1.call-start
  8.7 32.7 %reduce-scatter.7.cloned.1.call-done = bf16[1,224,576]{2,1,0:T(8,128)(2,1)} async-done(((bf16[4,224,576]{2,1,0:T(8,128)(2,1)}), bf16[1,224,576]{2,1,0:T(8,128)(2,1)}) %reduce-scatter.7.cloned.1.call-update) | async-done | bytes 258064
  41.4 0.0 copy-done.8
  41.4 2.5 multiply_reduce_fusion.1
  43.9 0.0 copy-start.9
  43.9 0.0 copy-start.13
  43.9 35.7 %reduce-scatter.9.cloned.1.call-done = bf16[1,512,512]{2,1,0:T(8,128)(2,1)} async-done(((bf16[4,512,512]{2,1,0:T(8,128)(2,1)}), bf16[1,512,512]{2,1,0:T(8,128)(2,1)}) %reduce-scatter.9.cloned.1.call-update) | async-done | bytes 524304
  79.6 0.0 copy-done.6
  79.6 1.9 multiply_reduce_fusion
  81.5 39.0 %all-reduce.2 = (f32[]{:T(128)}, f32[]{:T(128)}) all-reduce(f32[]{:T(128)} %get-tuple-element.16, f32[]{:T(128)} %get-tuple-element.14), channel_id=1, replica_groups=mesh['dp'=4,'mp'=8] {'dp','mp'}, use_global_device_ids=true, to_apply=%region_2.0 | all-reduce | flops 2 | bytes 16 | tf_op jit(solution)/shard_map/psum | solution.py:57
  121.9 0.0 copy-done.9
  121.9 0.0 copy-done.13
  121.9 2.8 fusion.35
  124.7 0.0 copy-done.10
  124.7 3.0 fusion.32
  127.7 0.0 all-reduce.14.cloned.1.call-update
  127.7 0.2 all-reduce.12.cloned.1.call-start
  127.9 136.5 %all-reduce.14.cloned.1.call-done = (f32[576,576]{1,0:T(8,128)}, f32[512,512]{1,0:T(8,128)}) async-done(((f32[576,576]{1,0:T(8,128)}, f32[512,512]{1,0:T(8,128)}), (f32[576,576]{1,0:T(8,128)}, f32[512,512]{1,0:T(8,128)})) %all-reduce.14.cloned.1.call-update) | async-done | bytes 2375696 | tf_op jit(solution)/shard_map/psum | solution.py:66
  264.4 6.2 fusion.48
  270.6 0.0 copy-done.2
  270.7 1.9 fusion.15
  272.6 0.0 copy-start.3
  272.6 2.7 fusion.49
  275.4 0.0 copy-done.3
  275.4 1.9 fusion.14
  277.3 0.0 copy-done.7
  277.3 2.0 convolution_add_fusion.2
  279.3 3.1 fusion.53
  282.4 0.0 all-reduce.12.cloned.1.call-update
  282.4 0.0 all-reduce.10.cloned.1.call-start
  282.4 135.1 %all-reduce.12.cloned.1.call-done = (f32[576,576]{1,0:T(8,128)}, f32[512,512]{1,0:T(8,128)}) async-done(((f32[576,576]{1,0:T(8,128)}, f32[512,512]{1,0:T(8,128)}), (f32[576,576]{1,0:T(8,128)}, f32[512,512]{1,0:T(8,128)})) %all-reduce.12.cloned.1.call-update) | async-done | bytes 2375696 | tf_op jit(solution)/shard_map/psum | solution.py:66
  417.5 6.2 fusion.50
  423.8 0.0 copy-done.1
  423.8 1.9 fusion.18
  425.6 0.0 copy-start.4
  425.7 2.7 fusion.51
  428.4 0.0 copy-done.4
  428.4 1.9 fusion.13
  430.3 1.8 convolution_add_fusion.1
  432.1 3.1 fusion.54
  435.3 0.0 all-reduce.10.cloned.1.call-update
  435.3 0.0 all-gather.4.cloned.1.call-start
  435.3 135.1 %all-reduce.10.cloned.1.call-done = (f32[576,576]{1,0:T(8,128)}, f32[512,512]{1,0:T(8,128)}) async-done(((f32[576,576]{1,0:T(8,128)}, f32[512,512]{1,0:T(8,128)}), (f32[576,576]{1,0:T(8,128)}, f32[512,512]{1,0:T(8,128)})) %all-reduce.10.cloned.1.call-update) | async-done | bytes 2375696 | tf_op jit(solution)/shard_map/psum | solution.py:66
  570.4 4.0 fusion.12
  574.4 0.0 copy-done.11
  574.4 0.0 copy-start
  574.4 3.2 broadcast_multiply_fusion
  577.6 0.0 all-gather.4.cloned.1.call-update
  577.6 0.0 copy-done
  577.6 0.0 copy-start.12
  577.6 4.2 fusion.52
  581.8 0.0 copy-done.12
  581.8 2.8 broadcast_multiply_fusion.1
  584.6 17.3 %all-gather = bf16[896,576]{1,0:T(8,128)(2,1)S(1)} all-gather(bf16[224,576]{1,0:T(8,128)(2,1)S(1)} %get-tuple-element.21), channel_id=2, replica_groups=mesh['dp'=4,'mp'=8] {'dp'}, dimensions={0}, use_global_device_ids=true | all-gather | bytes 1290240 | tf_op jit(solution)/shard_map/all_gather | solution.py:74
  601.9 14.8 %all-gather.4.cloned.1.call-done = bf16[2048,512]{1,0:T(8,128)(2,1)} async-done(((bf16[512,512]{1,0:T(8,128)(2,1)}), bf16[2048,512]{1,0:T(8,128)(2,1)}) %all-gather.4.cloned.1.call-update) | async-done | bytes 2097168 | tf_op jit(solution)/shard_map/all_gather | solution.py:75
  616.7 1.0 copy.20
  617.7 1.0 copy-done.5
  618.7 1.3 copy.21
  (6 shorter events, 0.0 us)
Async XLA Ops:
  7.2 34.2 %reduce-scatter.7.cloned.1.call-start = ((), (), s32[]{:S(2)}) async-start(), calls=%async_computation.3 | async-start | bytes 1433600
  7.2 34.2 %copy-start.8 = (f32[224,576]{1,0:T(8,128)S(1)}, f32[224,576]{1,0:T(8,128)}, u32[]{:S(2)}) copy-start(f32[224,576]{1,0:T(8,128)} %param.7) | copy-start | bytes 1548292
  7.9 71.7 %reduce-scatter.9.cloned.1.call-start = ((), (), s32[]{:S(2)}) async-start(), calls=%async_computation.4 | async-start | bytes 2621440
  7.9 71.6 %copy-start.6 = (f32[512,512]{1,0:T(8,128)S(1)}, f32[512,512]{1,0:T(8,128)}, u32[]{:S(2)}) copy-start(f32[512,512]{1,0:T(8,128)} %param.10) | copy-start | bytes 3145732
  8.6 255.7 %all-reduce.14.cloned.1.call-start = ((), (), s32[]{:S(2)}) async-start(), calls=%async_computation.7 | async-start | bytes 5046272 | tf_op jit(solution)/shard_map/psum | solution.py:66
  43.9 78.0 %copy-start.9 = (f32[224,576]{1,0:T(8,128)S(1)}, f32[224,576]{1,0:T(8,128)}, u32[]{:S(2)}) copy-start(f32[224,576]{1,0:T(8,128)} %get-tuple-element.29) | copy-start | bytes 1548292
  43.9 78.0 %copy-start.13 = (bf16[1,224,576]{2,1,0:T(8,128)(2,1)S(1)}, bf16[1,224,576]{2,1,0:T(8,128)(2,1)}, u32[]{:S(2)}) copy-start(bf16[1,224,576]{2,1,0:T(8,128)(2,1)} %reduce-scatter.7.cloned.1.call-done) | copy-start | bytes 774148
  81.5 195.8 %copy-start.7 = (f32[512,512]{1,0:T(8,128)}, f32[512,512]{1,0:T(8,128)S(1)}, u32[]{:S(2)}) copy-start(f32[512,512]{1,0:T(8,128)S(1)} %get-tuple-element.32) | copy-start | bytes 3145732
  81.5 43.2 %copy-start.10 = (bf16[1,512,512]{2,1,0:T(8,128)(2,1)S(1)}, bf16[1,512,512]{2,1,0:T(8,128)(2,1)}, u32[]{:S(2)}) copy-start(bf16[1,512,512]{2,1,0:T(8,128)(2,1)} %reduce-scatter.9.cloned.1.call-done) | copy-start | bytes 1572868
  127.7 289.8 %all-reduce.12.cloned.1.call-start = ((), (), s32[]{:S(2)}) async-start(), calls=%async_computation.6 | async-start | bytes 5046272 | tf_op jit(solution)/shard_map/psum | solution.py:66
  264.4 6.3 copy-start.2
  272.6 2.7 copy-start.3
  282.4 288.0 %all-reduce.10.cloned.1.call-start = ((), (), s32[]{:S(2)}) async-start(), calls=%async_computation.5 | async-start | bytes 5046272 | tf_op jit(solution)/shard_map/psum | solution.py:66
  417.5 6.3 copy-start.1
  425.6 2.7 copy-start.4
  435.3 181.5 %all-gather.4.cloned.1.call-start = ((), (), s32[]{:S(2)}) async-start(), calls=%async_computation.2 | async-start | bytes 2621440 | tf_op jit(solution)/shard_map/all_gather | solution.py:75
  570.4 4.0 copy-start.11
  574.4 3.2 copy-start
  577.6 4.2 copy-start.12
  616.7 2.0 copy-start.5
Sparse Core Ops, SparseCore 0:
  10.9 30.4 reduce-scatter.6
  44.4 35.1 reduce-scatter.8
  127.8 136.5 all-reduce.13
  282.5 134.9 all-reduce.11
  435.4 134.9 all-reduce.9
  577.7 38.9 all-gather.3
where the time goes:
time: 632 us; the launch traced here: 627 us
  waiting for transfers between devices  491 us (78%)
  blocking collectives  56.3 us (9%)
  matrix products  55.5 us (9%)
  between operations  16.1 us (3%)
    psum x3, waiting for transfers between devices, local(): lax.psum((gram_of(iterates[0]), gram_of(iterates[1])), ('dp', 'mp'))  407 us
    unnamed x8, waiting for transfers between devices  69.8 us
    psum x1, blocking collectives, local(): lax.psum((jnp.sum(directions[0] * directions[0]), jnp.sum(directions[1] *...  39 us
    dot_general x6, matrix products, newton(): jnp.dot(gram_matrix, gram_matrix, precision=PRECISE, preferred_element_ty...  24.4 us
    dot_general x6, matrix products, gram_of(): jnp.dot(value.T, value, precision=PRECISE, preferred_element_type=jnp.flo...  17.5 us
    all_gather x1, blocking collectives, local(): lax.all_gather(new_rows[0][None], 'dp', axis=0, tiled=True)  17.3 us
    all_gather x1, waiting for transfers between devices, local(): lax.all_gather(new_rows[1][None], 'dp', axis=0, tiled=True)  14.8 us
    dot_general x6, matrix products, newton(): jnp.dot(iterate, polynomial, precision=PRECISE, preferred_element_type=jn...  13.6 us
  transfers between devices with their start and end apart: 6, of which 6 were waited for; matrix products, arithmetic and copies ran while one was open for 2% of the time, Pallas kernels for 0%

commit v1 on v0

v1 whole, which is shorter than its diff:
```python
import functools
import math

import jax
import jax.numpy as jnp
from jax import lax
from jax.experimental import pallas as pl
from jax.experimental.pallas import tpu as pltpu
from jax.sharding import PartitionSpec as P

D = 7168
KEY_VALUE_ROWS = 16384
ITERS = 3

COEF_A = 3.4445
COEF_B = -4.775
COEF_C = 2.0315
MOMENT = 0.95
RATE = 0.2
DECAY = 0.1
EPSILON = 1e-07
MESH = pl.DeviceIdType.MESH
F32 = jnp.float32
BF16 = jnp.bfloat16
BLOCK = 128


def block_list(columns):
    count = -(-columns // BLOCK)
    return [(i, j) for i in range(count) for j in range(i, count)]


def split(value):
    high = value.astype(BF16)
    return high, (value - high.astype(F32)).astype(BF16)


def partners(dp, mp):
    d, m = lax.axis_index("dp"), lax.axis_index("mp")
    core = lax.rem(m, 2)
    sibling = (d, m + 1 - 2 * core)
    group = [(lax.rem(d + r, dp), m) for r in range(1, dp)]
    line = [(d, lax.rem(m + 2 * r, mp)) for r in range(1, mp // 2)]
    return d, m, core, sibling, group, line


def greet(others):
    barrier = pltpu.get_barrier_semaphore()
    for other in others:
        pl.semaphore_signal(barrier, inc=1, device_id=other, device_id_type=MESH)
    pl.semaphore_wait(barrier, len(others))


def remote(src, dst, send, recv, target):
    return pltpu.make_async_remote_copy(
        src_ref=src, dst_ref=dst, send_sem=send, recv_sem=recv, device_id=target, device_id_type=MESH
    )


def gather_rows(start, size):
    return pl.ds(pl.multiple_of(start, 8), size)


def reduce_kernel(
    dp, mp, total,
    grads_a, grads_b, mom_a, mom_b,
    new_a, new_b, dir_a, dir_b, gram_a, gram_b,
    own_a, own_b, got_a, got_b, wide_a, pack, half, quarter, part, red, quart_recv, part_recv,
    own_sem, rs_send, rs_recv, core_sem, dp_send, dp_recv, line_send, line_recv, line_send2, line_recv2,
    dp_send2, dp_recv2,
):
    d, m, core, sibling, group, line = partners(dp, mp)
    z = m // 2
    zn = mp // 2
    half_rows = total // 2
    quarter_rows = half_rows // dp
    part_rows = quarter_rows // zn
    locals_ = [
        pltpu.make_async_copy(grads_b.at[0, d], own_b, own_sem.at[0]),
        pltpu.make_async_copy(grads_a.at[0, d], own_a, own_sem.at[1]),
    ]
    for copy in locals_:
        copy.start()
    greet([sibling] + group + line)
    scatter = [[], []]
    for which, (grads, got) in enumerate(((grads_b, got_b), (grads_a, got_a))):
        for r in range(1, dp):
            target = group[r - 1]
            copy = remote(
                grads.at[0, target[0]], got.at[r - 1],
                rs_send.at[which, r - 1], rs_recv.at[which, r - 1], target,
            )
            copy.start()
            scatter[which].append(copy)

    used = (len(block_list(gram_a.shape[0])) + len(block_list(gram_b.shape[0]))) * BLOCK
    if total > used:
        pack[pl.ds(used, total - used), :] = jnp.zeros((total - used, BLOCK), F32)
    offset_a = len(block_list(gram_b.shape[0])) * BLOCK

    for which, (own, got, mom, new, direction) in enumerate(
        ((own_b, got_b, mom_b, new_b, dir_b), (own_a, got_a, mom_a, new_a, dir_a))
    ):
        locals_[which].wait()
        for copy in scatter[which]:
            copy.wait_recv()
        summed = own[...].astype(F32)
        for r in range(dp - 1):
            summed = summed + got[r].astype(F32)
        state = MOMENT * mom[...] + summed
        new[...] = state
        value = summed + MOMENT * state
        direction[...] = value
        columns = value.shape[1]
        count = -(-columns // BLOCK)
        if columns % BLOCK:
            wide_a[...] = jnp.zeros(wide_a.shape, F32)
            wide_a[:, :columns] = value
            value = wide_a[...]
        high, low = split(value)
        at = offset_a if which else 0
        for i in range(count):
            left = slice(i * BLOCK, (i + 1) * BLOCK)
            right = slice(i * BLOCK, count * BLOCK)

            def product(x, y):
                return lax.dot_general(x, y, (((0,), (0,)), ((), ())), preferred_element_type=F32)

            row = (
                product(high[:, left], high[:, right])
                + product(high[:, left], low[:, right])
                + product(low[:, left], high[:, right])
            )
            for j in range(count - i):
                pack[at : at + BLOCK, :] = row[:, j * BLOCK : (j + 1) * BLOCK]
                at += BLOCK
    core_copy = remote(
        pack.at[gather_rows((1 - core) * half_rows, half_rows)], half, core_sem.at[0], core_sem.at[1], sibling
    )
    core_copy.start()
    core_copy.wait()
    half[...] = half[...] + pack[gather_rows(core * half_rows, half_rows), :]
    copies = []
    for r in range(1, dp):
        target = group[r - 1]
        copy = remote(
            half.at[gather_rows(target[0] * quarter_rows, quarter_rows)], quart_recv.at[r - 1],
            dp_send.at[r - 1], dp_recv.at[r - 1], target,
        )
        copy.start()
        copies.append(copy)
    value = half[gather_rows(d * quarter_rows, quarter_rows), :]
    for r, copy in enumerate(copies):
        copy.wait_recv()
        value = value + quart_recv[r]
    quarter[...] = value
    line_copies = []
    for r in range(1, zn):
        target = line[r - 1]
        copy = remote(
            quarter.at[gather_rows((target[1] // 2) * part_rows, part_rows)], part_recv.at[r - 1],
            line_send.at[r - 1], line_recv.at[r - 1], target,
        )
        copy.start()
        line_copies.append(copy)
    value = quarter[gather_rows(z * part_rows, part_rows), :]
    for r, copy in enumerate(line_copies):
        copy.wait_recv()
        value = value + part_recv[r]
    my_quarter = core * half_rows + d * quarter_rows
    my_part = my_quarter + z * part_rows
    red[gather_rows(my_part, part_rows), :] = value
    back = []
    for r in range(1, zn):
        spot = red.at[gather_rows(my_part, part_rows)]
        copy = remote(spot, spot, line_send2.at[r - 1], line_recv2.at[r - 1], line[r - 1])
        copy.start()
        back.append(copy)
    for copy in back:
        copy.wait_recv()
    back_dp = []
    for r in range(1, dp):
        spot = red.at[gather_rows(my_quarter, quarter_rows)]
        copy = remote(spot, spot, dp_send2.at[r - 1], dp_recv2.at[r - 1], group[r - 1])
        copy.start()
        back_dp.append(copy)
    for copy in back_dp:
        copy.wait_recv()
    spot = red.at[gather_rows(core * half_rows, half_rows)]
    core_back = remote(spot, spot, core_sem.at[2], core_sem.at[3], sibling)
    core_back.start()
    for copy in scatter[0] + scatter[1] + copies + line_copies + back + back_dp:
        copy.wait_send()
    core_back.wait()
    at = 0
    for gram in (gram_b, gram_a):
        columns = gram.shape[0]
        for i, j in block_list(columns):
            block = red[at : at + BLOCK, :]
            at += BLOCK
            rows_end = min((i + 1) * BLOCK, columns)
            cols_end = min((j + 1) * BLOCK, columns)
            high_rows, wide = rows_end - i * BLOCK, cols_end - j * BLOCK
            gram[i * BLOCK : rows_end, j * BLOCK : cols_end] = block[:high_rows, :wide]
            if i != j:
                gram[j * BLOCK : cols_end, i * BLOCK : rows_end] = block.T[:wide, :high_rows]


def reduce_call(dp, mp, grads_a, grads_b, mom_a, mom_b):
    ra, ca = mom_a.shape
    rb, cb = mom_b.shape
    unit = 8 * dp * mp
    used = (len(block_list(ca)) + len(block_list(cb))) * BLOCK
    total = -(-used // unit) * unit
    zn = mp // 2
    half_rows = total // 2
    quarter_rows = half_rows // dp
    part_rows = quarter_rows // zn
    vmem = pl.BlockSpec(memory_space=pltpu.VMEM)
    hbm = pl.BlockSpec(memory_space=pl.ANY)
    shape = jax.ShapeDtypeStruct
    sem = pltpu.SemaphoreType.DMA
    wide = -(-ca // BLOCK) * BLOCK
    return pl.pallas_call(
        functools.partial(reduce_kernel, dp, mp, total),
        out_shape=[
            shape((ra, ca), F32), shape((rb, cb), F32),
            shape((ra, ca), F32), shape((rb, cb), F32),
            shape((ca, ca), F32), shape((cb, cb), F32),
        ],
        in_specs=[hbm, hbm, vmem, vmem],
        out_specs=[vmem] * 6,
        scratch_shapes=[
            pltpu.VMEM((ra, ca), BF16),
            pltpu.VMEM((rb, cb), BF16),
            pltpu.VMEM((dp - 1, ra, ca), BF16),
            pltpu.VMEM((dp - 1, rb, cb), BF16),
            pltpu.VMEM((ra, wide), F32),
            pltpu.VMEM((total, BLOCK), F32),
            pltpu.VMEM((half_rows, BLOCK), F32),
            pltpu.VMEM((quarter_rows, BLOCK), F32),
            pltpu.VMEM((part_rows, BLOCK), F32),
            pltpu.VMEM((total, BLOCK), F32),
            pltpu.VMEM((dp - 1, quarter_rows, BLOCK), F32),
            pltpu.VMEM((zn - 1, part_rows, BLOCK), F32),
            sem((2,)),
            sem((2, dp - 1)),
            sem((2, dp - 1)),
            sem((4,)),
            sem((dp - 1,)),
            sem((dp - 1,)),
            sem((zn - 1,)),
            sem((zn - 1,)),
            sem((zn - 1,)),
            sem((zn - 1,)),
            sem((dp - 1,)),
            sem((dp - 1,)),
        ],
        compiler_params=pltpu.CompilerParams(
            collective_id=0, has_side_effects=True, vmem_limit_bytes=40 * 2**20
        ),
    )(grads_a, grads_b, mom_a, mom_b)


def spread_kernel(dp, rows_a, rows_b, out_a, out_b, own_sem, send, recv):
    d, m = lax.axis_index("dp"), lax.axis_index("mp")
    low, high = lax.rem(d, 2), d // 2
    near = (d + 1 - 2 * low, m)
    far = (lax.rem(d + 2, 4), m)
    mine = [
        pltpu.make_async_copy(rows_b, out_b.at[d], own_sem.at[0]),
        pltpu.make_async_copy(rows_a, out_a.at[d], own_sem.at[1]),
    ]
    for copy in mine:
        copy.start()
    greet([near, far])
    first = {}
    for which, (rows, out) in enumerate(((rows_b, out_b), (rows_a, out_a))):
        for side, target in enumerate((near, far)):
            copy = remote(rows, out.at[d], send.at[which, side], recv.at[which, side], target)
            copy.start()
            first[which, side] = copy
    later = []
    for which, (rows, out) in enumerate(((rows_b, out_b), (rows_a, out_a))):
        count = rows.shape[0]
        cut = count // 2 // 16 * 16
        for side, (source, target, start, size) in enumerate(
            ((near[0], far, 0, cut), (far[0], near, cut, count - cut))
        ):
            first[which, side].wait_recv()
            if size:
                spot = out.at[source] if size == count else out.at[source, pl.ds(start, size)]
                copy = remote(spot, spot, send.at[which, 2 + side], recv.at[which, 2 + side], target)
                copy.start()
                later.append(copy)
    for copy in mine:
        copy.wait()
    for copy in first.values():
        copy.wait_send()
    for copy in later:
        copy.wait()


def spread_call(dp, rows_a, rows_b):
    hbm = pl.BlockSpec(memory_space=pl.ANY)
    sem = pltpu.SemaphoreType.DMA
    return pl.pallas_call(
        functools.partial(spread_kernel, dp),
        out_shape=[
            jax.ShapeDtypeStruct((dp,) + rows_a.shape, BF16),
            jax.ShapeDtypeStruct((dp,) + rows_b.shape, BF16),
        ],
        in_specs=[hbm, hbm],
        out_specs=[hbm, hbm],
        scratch_shapes=[sem((2,)), sem((2, 4)), sem((2, 4))],
        compiler_params=pltpu.CompilerParams(collective_id=1, has_side_effects=True),
    )(rows_a, rows_b)


def times(x, y):
    return jnp.dot(x, y, precision=lax.Precision.HIGH, preferred_element_type=F32)


def orthogonal(direction, gram):
    scale = 1.0 / (jnp.sqrt(jnp.trace(gram)) + EPSILON)
    iterate = direction * scale
    gram = gram * scale * scale
    for step in range(ITERS):
        poly = COEF_B * gram + COEF_C * times(gram, gram)
        if step < ITERS - 1:
            inner = COEF_A * gram + times(gram, poly)
            gram = COEF_A * inner + times(poly, inner)
        iterate = COEF_A * iterate + times(iterate, poly)
    return iterate


def local(dp, mp, grads_a, momentum_a, weights_a, up_gradient_parts, up_momentum_buffer, up_weight_before):
    new_a, new_b, dir_a, dir_b, gram_a, gram_b = reduce_call(
        dp, mp, grads_a, up_gradient_parts, momentum_a, up_momentum_buffer
    )
    update_a = 0.2 * math.sqrt(D) * orthogonal(dir_a, gram_a)
    update_b = 0.2 * math.sqrt(KEY_VALUE_ROWS) * orthogonal(dir_b, gram_b)
    rows_a = (weights_a.astype(F32) * (1.0 - RATE * DECAY) - RATE * update_a).astype(BF16)
    rows_b = (up_weight_before.astype(F32) * (1.0 - RATE * DECAY) - RATE * update_b).astype(BF16)
    weight_a, weight_b = spread_call(dp, rows_a, rows_b)
    return (weight_a, new_a, update_a, weight_b, new_b, update_b)


def solution(mesh):
    both = P(("dp", "mp"), None)
    grads = P("dp", None, "mp", None)
    weights = P(None, "mp", None)
    return jax.shard_map(
        functools.partial(local, mesh.shape["dp"], mesh.shape["mp"]),
        mesh=mesh,
        in_specs=(grads, both, both, grads, both, both),
        out_specs=(weights, both, both, weights, both, both),
        check_vma=False,
    )
```

time: 632 us -> 160 us (0.25)
  waiting for transfers between devices: 491 us -> 0 us
  Pallas kernels: 0 us -> 108 us
  blocking collectives: 56.3 us -> 0 us
  matrix products: 55.5 us -> 32.4 us
  between operations: 16.1 us -> 2.33 us
  local copies, waits for them, and re-layouts: 3.38 us -> 14.3 us
    psum x3 -> x0, waiting for transfers between devices: 407 us -> none  [local(): lax.psum((gram_of(iterates[0]), gram_of(iterates[1])), ('dp', 'mp'))]
    pallas_call x0 -> x2, Pallas kernels: none -> 108 us  [the longest x1 79.1 us: reduce_call(): pl.pallas_call(functools.partial(reduce_kernel, dp, mp, total), out_shape...]
    unnamed x8 -> x0, waiting for transfers between devices: 69.8 us -> none
    psum x1 -> x0, blocking collectives: 39 us -> none  [local(): lax.psum((jnp.sum(directions[0] * directions[0]), jnp.sum(directions[1] *...]
    dot_general x18 -> x20, matrix products: 55.5 us -> 32.4 us  [times(): jnp.dot(x, y, precision=lax.Precision.HIGH, preferred_element_type=F32)]
    all_gather x1 -> x0, blocking collectives: 17.3 us -> none  [local(): lax.all_gather(new_rows[0][None], 'dp', axis=0, tiled=True)]
    all_gather x1 -> x0, waiting for transfers between devices: 14.8 us -> none  [local(): lax.all_gather(new_rows[1][None], 'dp', axis=0, tiled=True)]
    unnamed x30, local copies, waits for them, and re-layouts: 3.38 us -> 14.3 us
  transfers between devices with their start and end apart: 6 -> 0, of which waited for: 6 -> 0; matrix products, arithmetic and copies ran while one was open for 2% -> 0% of each run, Pallas kernels for 0% -> 0%
where the time goes in v1:
time: 160 us; the launch traced here: 159 us
  Pallas kernels  108 us (68%)
  matrix products  32.4 us (20%)
  local copies, waits for them, and re-layouts  14.3 us (9%)
  between operations  2.33 us (1%)
    pallas_call x1, Pallas kernels, reduce_call(): pl.pallas_call(functools.partial(reduce_kernel, dp, mp, total), out_shape...  79.1 us
    dot_general x20, matrix products, times(): jnp.dot(x, y, precision=lax.Precision.HIGH, preferred_element_type=F32)  32.4 us
    pallas_call x1, Pallas kernels, spread_call(): pl.pallas_call(functools.partial(spread_kernel, dp), out_shape=[jax.Shape...  29.2 us
    unnamed x30, local copies, waits for them, and re-layouts  14.3 us

profile of v1, /device:TPU:1, one launch (start us, length us, event | category | flops | bytes accessed | tf_op | source)
XLA Modules:
  0.0 158.7 jit_solution(11197823224188345610)
XLA Ops:
  0.6 0.0 copy-start
  0.6 1.6 copy-done
  2.2 0.0 copy-start.1
  2.2 1.3 copy-done.1
  3.5 0.0 copy-start.2
  3.5 1.2 copy-done.2
  4.7 0.0 copy-start.7
  4.7 1.1 copy-done.7
  5.8 79.1 %shard_map.109 = (f32[224,576]{1,0:T(8,128)S(1)}, f32[512,512]{1,0:T(8,128)S(1)}, f32[224,576]{1,0:T(8,128)S(1)}, f32[512,512]{1,0:T(8,128)S(1)}, f32[576,576]{1,0:T(8,128)S(1)}, /*index=5*/f32[512,512]{1,0:T(8,128)S(1)}) custom-call(bf16[1,4,224,576]{3,2,1,0:T(8,128)(2,1)S(1)} %copy-done.1, bf16[1,4,512,512]{3,2,1,0:T(8,128)(2,1)S(1)} %copy-done, ...), custom_call_target="tpu_custom_call" | custom-call | tf_op jit(solution)/shard_map/pallas_call | solution.py:224
  84.8 0.0 copy-start.3
  84.8 1.0 copy-done.3
  85.8 0.0 copy-start.5
  85.9 1.0 copy-done.5
  86.8 0.0 copy-start.8
  86.8 0.8 copy-done.8
  87.6 0.7 select_reduce_fusion
  89.0 0.7 select_reduce_fusion.1
  90.4 1.1 fusion.18
  91.5 0.0 copy-start.6
  91.6 1.1 convolution_add_fusion.5
  92.6 0.2 copy-done.6
  92.8 1.0 convolution_add_fusion.6
  93.8 1.0 convolution_add_fusion.4
  94.8 1.0 fusion.17
  95.9 1.0 convolution_add_fusion.2
  96.9 1.0 convolution_add_fusion.1
  97.9 1.0 convolution_add_fusion.3
  98.9 0.0 copy-start.11
  98.9 1.0 fusion.16
  100.0 0.0 copy-done.11
  100.0 2.5 %broadcast_multiply_fusion = (f32[512,512]{1,0:T(8,128)}, bf16[512,512]{1,0:T(8,128)(2,1)}) fusion(bf16[512,512]{1,0:T(8,128)(2,1)S(1)} %copy-done.11, f32[512,512]{1,0:T(8,128)S(1)} %convolution_add_fusion.3, f32[512,512]{1,0:T(8,128)S(1)} %fusion.16), kind=kOutput, calls=%fused_computation.67 | convolution fusion | flops 807403520 | bytes 4194304 | tf_op jit(solution)/shard_map/dot_general | solution.py:321
  102.5 2.2 %fusion.25 = f32[576,576]{1,0:T(8,128)S(1)} fusion(f32[576,576]{1,0:T(8,128)S(1)} %get-tuple-element.15, f32[]{:T(128)S(6)} %div.6), kind=kOutput, calls=%fused_computation.46 | convolution fusion | flops 1147281408 | bytes 2654212 | tf_op jit(solution)/shard_map/dot_general | solution.py:321
  104.7 1.1 fusion.19
  105.9 2.4 %multiply_add_fusion.11 = f32[576,576]{1,0:T(8,128)S(1)} fusion(f32[576,576]{1,0:T(8,128)S(1)} %fusion.25, f32[576,576]{1,0:T(8,128)S(1)} %get-tuple-element.15, f32[]{:T(128)S(6)} %div.6), kind=kOutput, calls=%fused_computation.14 | convolution fusion | flops 1150267392 | bytes 3981316 | tf_op jit(solution)/shard_map/dot_general | solution.py:321
  108.2 2.4 %multiply_add_fusion.10 = f32[576,576]{1,0:T(8,128)S(1)} fusion(f32[576,576]{1,0:T(8,128)S(1)} %multiply_add_fusion.11, f32[576,576]{1,0:T(8,128)S(1)} %fusion.25, f32[576,576]{1,0:T(8,128)S(1)} %get-tuple-element.15, f32[]{:T(128)S(6)} %div.6), kind=kOutput, calls=%fused_computation.13 | convolution fusion | flops 1148940288 | bytes 5308420 | tf_op jit(solution)/shard_map/dot_general | solution.py:321
  110.6 2.2 %fusion.63 = f32[576,576]{1,0:T(8,128)S(1)} fusion(f32[576,576]{1,0:T(8,128)S(1)} %multiply_add_fusion.10), kind=kOutput, calls=%fused_computation.87 | convolution fusion | flops 1146617856 | bytes 2654208 | tf_op jit(solution)/shard_map/dot_general | solution.py:321
  112.9 1.1 fusion.20
  114.0 2.5 %multiply_add_fusion.1 = f32[576,576]{1,0:T(8,128)S(1)} fusion(f32[576,576]{1,0:T(8,128)S(1)} %multiply_add_fusion.10, f32[576,576]{1,0:T(8,128)S(1)} %fusion.63), kind=kOutput, calls=%fused_computation.5 | convolution fusion | flops 1148276736 | bytes 3981312 | tf_op jit(solution)/shard_map/dot_general | solution.py:321
  116.5 2.4 %multiply_add_fusion = f32[576,576]{1,0:T(8,128)S(1)} fusion(f32[576,576]{1,0:T(8,128)S(1)} %multiply_add_fusion.1, f32[576,576]{1,0:T(8,128)S(1)} %fusion.63, f32[576,576]{1,0:T(8,128)S(1)} %multiply_add_fusion.10), kind=kOutput, calls=%fused_computation.4 | convolution fusion | flops 1148276736 | bytes 5308416 | tf_op jit(solution)/shard_map/dot_general | solution.py:321
  118.9 0.0 copy-start.12
  118.9 2.2 %fusion.64 = f32[576,576]{1,0:T(8,128)S(1)} fusion(f32[576,576]{1,0:T(8,128)S(1)} %multiply_add_fusion), kind=kOutput, calls=%fused_computation.88 | convolution fusion | flops 1146617856 | bytes 2654208 | tf_op jit(solution)/shard_map/dot_general | solution.py:321
  121.1 0.0 copy-done.12
  121.1 2.1 %broadcast_multiply_fusion.1 = (f32[224,576]{1,0:T(8,128)}, bf16[224,576]{1,0:T(8,128)(2,1)}) fusion(bf16[224,576]{1,0:T(8,128)(2,1)S(1)} %copy-done.12, f32[224,576]{1,0:T(8,128)S(1)} %fusion.20, f32[576,576]{1,0:T(8,128)S(1)} %fusion.64, f32[576,576]{1,0:T(8,128)S(1)} %multiply_add_fusion), kind=kOutput, calls=%fused_computation.71 | convolution fusion | flops 447934464 | bytes 4202496 | tf_op jit(solution)/shard_map/dot_general | solution.py:321
  123.2 0.0 copy-start.9
  123.2 29.2 %shard_map.110 = (bf16[4,224,576]{2,1,0:T(8,128)(2,1)}, bf16[4,512,512]{2,1,0:T(8,128)(2,1)}) custom-call(bf16[224,576]{1,0:T(8,128)(2,1)} %get-tuple-element.25.rows_a, bf16[512,512]{1,0:T(8,128)(2,1)} %get-tuple-element.23.rows_b), custom_call_target="tpu_custom_call" | custom-call | tf_op jit(solution)/shard_map/pallas_call | solution.py:307
  152.4 0.0 copy-start.10
  152.4 2.5 %copy.16 = bf16[4,224,576]{2,1,0:T(8,128)(2,1)} copy(bf16[4,224,576]{2,1,0:T(8,128)(2,1)} %get-tuple-element.32) | data formatting | bytes 2064384
  154.9 0.0 copy-done.9
  154.9 0.8 copy.17
  155.7 0.0 copy-done.10
  155.7 0.0 copy-start.4
  155.7 1.3 copy.18
  157.1 0.6 copy-done.4
  157.7 1.0 copy.19
Async XLA Ops:
  0.6 1.6 %copy-start = (bf16[1,4,512,512]{3,2,1,0:T(8,128)(2,1)S(1)}, bf16[1,4,512,512]{3,2,1,0:T(8,128)(2,1)}, u32[]{:S(2)}) copy-start(bf16[1,4,512,512]{3,2,1,0:T(8,128)(2,1)} %grads_b.1) | copy-start | bytes 6291460
  2.2 1.3 copy-start.1
  3.5 1.2 copy-start.2
  4.7 1.1 copy-start.7
  84.8 1.0 copy-start.3
  85.8 1.0 copy-start.5
  86.8 0.8 copy-start.8
  91.5 1.2 copy-start.6
  98.9 1.1 copy-start.11
  118.9 2.3 %copy-start.12 = (bf16[224,576]{1,0:T(8,128)(2,1)S(1)}, bf16[224,576]{1,0:T(8,128)(2,1)}, u32[]{:S(2)}) copy-start(bf16[224,576]{1,0:T(8,128)(2,1)} %param.8) | copy-start | bytes 774148
  123.2 31.7 %copy-start.9 = (f32[224,576]{1,0:T(8,128)S(1)}, f32[224,576]{1,0:T(8,128)}, u32[]{:S(2)}) copy-start(f32[224,576]{1,0:T(8,128)} %copy-done.8) | copy-start | bytes 1548292
  152.4 3.3 %copy-start.10 = (bf16[4,512,512]{2,1,0:T(8,128)(2,1)S(1)}, bf16[4,512,512]{2,1,0:T(8,128)(2,1)}, u32[]{:S(2)}) copy-start(bf16[4,512,512]{2,1,0:T(8,128)(2,1)} %get-tuple-element.35) | copy-start | bytes 6291460
  155.7 2.0 %copy-start.4 = (f32[512,512]{1,0:T(8,128)S(1)}, f32[512,512]{1,0:T(8,128)}, u32[]{:S(2)}) copy-start(f32[512,512]{1,0:T(8,128)} %copy-done.3) | copy-start | bytes 3145732

commit v2 on v0

v2 whole, which is shorter than its diff:
```python
import functools
import math

import jax
import jax.numpy as jnp
from jax import lax
from jax.experimental import pallas as pl
from jax.experimental.pallas import tpu as pltpu
from jax.sharding import PartitionSpec as P

D = 7168
KEY_VALUE_ROWS = 16384
ITERS = 3

COEF_A = 3.4445
COEF_B = -4.775
COEF_C = 2.0315
MOMENT = 0.95
RATE = 0.2
DECAY = 0.1
EPSILON = 1e-07
MESH = pl.DeviceIdType.MESH
F32 = jnp.float32
BF16 = jnp.bfloat16
BLOCK = 128
TILE = 256


def padded(columns):
    return -(-columns // BLOCK) * BLOCK


def block_list(columns):
    count = padded(columns) // BLOCK
    return [(i, j) for i in range(count) for j in range(i, count)]


def packed_rows(columns, devices):
    unit = 8 * devices
    return -(-len(block_list(columns)) * BLOCK // unit) * unit


def split(value):
    high = value.astype(BF16)
    return high, (value - high.astype(F32)).astype(BF16)


def greet(others):
    barrier = pltpu.get_barrier_semaphore()
    for other in others:
        pl.semaphore_signal(barrier, inc=1, device_id=other, device_id_type=MESH)
    pl.semaphore_wait(barrier, len(others))


def remote(src, dst, send, recv, target):
    return pltpu.make_async_remote_copy(
        src_ref=src, dst_ref=dst, send_sem=send, recv_sem=recv, device_id=target, device_id_type=MESH
    )


def rows_at(start, size):
    return pl.ds(pl.multiple_of(start, 8), size)


class Side:
    def __init__(self, place, gain, grads, mom_in, old_in, out_weight, out_state, out_update, scratch):
        self.place, self.gain = place, gain
        self.grads, self.mom_in, self.old_in = grads, mom_in, old_in
        self.out_weight, self.out_state, self.out_update = out_weight, out_state, out_update
        (
            self.own, self.got, self.mom, self.old, self.state, self.update, self.rows, self.iterate,
            self.pack, self.half, self.quarter, self.part, self.red, self.quart_recv, self.part_recv,
            self.gram, self.poly, self.inner, self.left, self.right,
            self.in_sem, self.out_sem, self.rs_send, self.rs_recv, self.core_sem,
            self.dp_sem, self.line_sem, self.ag_send, self.ag_recv,
        ) = scratch
        self.d, self.m, self.core, self.sibling, self.group, self.line = place
        self.columns = self.mom.shape[1]
        self.wide = self.iterate.shape[1]
        self.z = self.m // 2
        self.total = self.pack.shape[0]
        self.half_rows = self.total // 2
        self.quarter_rows = self.quarter.shape[0]
        self.part_rows = self.part.shape[0]
        self.my_half = self.core * self.half_rows
        self.my_quarter = self.my_half + self.d * self.quarter_rows
        self.my_part = self.my_quarter + self.z * self.part_rows
        self.sent = []

    def load(self):
        self.loads = []
        for i, (src, dst) in enumerate(
            ((self.grads.at[0, self.d], self.own), (self.mom_in, self.mom), (self.old_in, self.old))
        ):
            copy = pltpu.make_async_copy(src, dst, self.in_sem.at[i])
            copy.start()
            self.loads.append(copy)

    def scatter(self):
        self.scattered = []
        for r, target in enumerate(self.group):
            copy = remote(
                self.grads.at[0, target[0]], self.got.at[r], self.rs_send.at[r], self.rs_recv.at[r], target
            )
            copy.start()
            self.scattered.append(copy)

    def scatter_sent(self):
        for copy in self.scattered:
            copy.wait_send()

    def local_gram(self):
        used = len(block_list(self.columns)) * BLOCK
        if self.total > used:
            self.pack[used:, :] = jnp.zeros((self.total - used, BLOCK), F32)
        if self.wide > self.columns:
            self.iterate[...] = jnp.zeros(self.iterate.shape, F32)
        for ref in (self.gram, self.poly, self.inner):
            if self.wide > self.columns:
                ref[...] = jnp.zeros(ref.shape, F32)
        for copy in self.loads:
            copy.wait()
        for copy in self.scattered:
            copy.wait_recv()
        summed = self.own[...].astype(F32)
        for r in range(len(self.group)):
            summed = summed + self.got[r].astype(F32)
        state = MOMENT * self.mom[...] + summed
        self.state[...] = state
        self.iterate[:, : self.columns] = summed + MOMENT * state
        self.outs = [pltpu.make_async_copy(self.state, self.out_state, self.out_sem.at[0])]
        self.outs[0].start()
        high, low = split(self.iterate[...])

        def product(x, y):
            return lax.dot_general(x, y, (((0,), (0,)), ((), ())), preferred_element_type=F32)

        at = 0
        count = self.wide // BLOCK
        for i in range(count):
            left, right = slice(i * BLOCK, (i + 1) * BLOCK), slice(i * BLOCK, count * BLOCK)
            row = (
                product(high[:, left], high[:, right])
                + product(high[:, left], low[:, right])
                + product(low[:, left], high[:, right])
            )
            for j in range(count - i):
                self.pack[at : at + BLOCK, :] = row[:, j * BLOCK : (j + 1) * BLOCK]
                at += BLOCK

    def start(self, copies):
        self.flying = copies
        for copy in copies:
            copy.start()

    def arrived(self):
        for copy in self.flying:
            copy.wait_recv()
        self.sent += self.flying

    def core_start(self):
        src = self.pack.at[rows_at((1 - self.core) * self.half_rows, self.half_rows)]
        self.start([remote(src, self.half, self.core_sem.at[0], self.core_sem.at[1], self.sibling)])

    def core_end(self):
        self.arrived()
        self.half[...] = self.half[...] + self.pack[rows_at(self.my_half, self.half_rows), :]

    def dp_start(self):
        self.start([
            remote(
                self.half.at[rows_at(target[0] * self.quarter_rows, self.quarter_rows)], self.quart_recv.at[r],
                self.dp_sem.at[0, r], self.dp_sem.at[1, r], target,
            )
            for r, target in enumerate(self.group)
        ])

    def dp_end(self):
        self.arrived()
        value = self.half[rows_at(self.d * self.quarter_rows, self.quarter_rows), :]
        for r in range(len(self.group)):
            value = value + self.quart_recv[r]
        self.quarter[...] = value

    def line_start(self):
        self.start([
            remote(
                self.quarter.at[rows_at((target[1] // 2) * self.part_rows, self.part_rows)], self.part_recv.at[r],
                self.line_sem.at[0, r], self.line_sem.at[1, r], target,
            )
            for r, target in enumerate(self.line)
        ])

    def line_end(self):
        self.arrived()
        value = self.quarter[rows_at(self.z * self.part_rows, self.part_rows), :]
        for r in range(len(self.line)):
            value = value + self.part_recv[r]
        self.red[rows_at(self.my_part, self.part_rows), :] = value

    def line_back(self):
        spot = self.red.at[rows_at(self.my_part, self.part_rows)]
        self.start([
            remote(spot, spot, self.line_sem.at[2, r], self.line_sem.at[3, r], target)
            for r, target in enumerate(self.line)
        ])

    def dp_back(self):
        spot = self.red.at[rows_at(self.my_quarter, self.quarter_rows)]
        self.start([
            remote(spot, spot, self.dp_sem.at[2, r], self.dp_sem.at[3, r], target)
            for r, target in enumerate(self.group)
        ])

    def core_back(self):
        spot = self.red.at[rows_at(self.my_half, self.half_rows)]
        self.start([remote(spot, spot, self.core_sem.at[2], self.core_sem.at[3], self.sibling)])

    def unpack(self):
        trace = jnp.zeros((1, 1), F32)
        diagonal = lax.broadcasted_iota(jnp.int32, (BLOCK, BLOCK), 0) == lax.broadcasted_iota(
            jnp.int32, (BLOCK, BLOCK), 1
        )
        for k, (i, j) in enumerate(block_list(self.columns)):
            if i == j:
                block = self.red[k * BLOCK : (k + 1) * BLOCK, :]
                trace = trace + jnp.sum(jnp.where(diagonal, block, 0.0), keepdims=True)
        scale = 1.0 / (jnp.sqrt(trace) + EPSILON)
        for k, (i, j) in enumerate(block_list(self.columns)):
            block = self.red[k * BLOCK : (k + 1) * BLOCK, :] * scale * scale
            up, down = slice(i * BLOCK, (i + 1) * BLOCK), slice(j * BLOCK, (j + 1) * BLOCK)
            self.gram[up, down] = block
            if i != j:
                self.gram[down, up] = block.T
        self.iterate[...] = self.iterate[...] * scale

    def set_left(self, value):
        high, low = split(value)
        self.left[:, : self.wide] = high
        self.left[:, self.wide : 2 * self.wide] = high
        self.left[:, 2 * self.wide :] = low

    def set_right(self, value):
        high, low = split(value)
        self.right[: self.wide, :] = high
        self.right[self.wide : 2 * self.wide, :] = low
        self.right[2 * self.wide :, :] = high

    def product(self, out, coefficient, base, base_coefficient):
        for at in range(0, self.wide, TILE):
            to = min(at + TILE, self.wide)
            cols = slice(at, to)
            value = jnp.dot(
                self.left[at : self.columns, :], self.right[:, cols], preferred_element_type=F32
            )
            out[at : self.columns, cols] = (
                base_coefficient * base[at : self.columns, cols] + coefficient * value
            )
            if to < self.wide:
                out[cols, to:] = out[to:, cols].T

    def newton(self, step):
        gram = self.gram[...]
        self.set_left(gram)
        self.set_right(gram)
        self.product(self.poly, COEF_C, self.gram, COEF_B)
        self.set_right(self.poly[...])
        value = self.iterate[...]
        high, low = split(value)
        self.iterate[...] = COEF_A * value + jnp.dot(
            jnp.concatenate([high, high, low], axis=1), self.right[...], preferred_element_type=F32
        )
        if step < ITERS - 1:
            self.product(self.inner, 1.0, self.gram, COEF_A)
            self.set_left(self.poly[...])
            self.set_right(self.inner[...])
            self.product(self.gram, 1.0, self.inner, COEF_A)

    def finish(self):
        update = self.gain * self.iterate[:, : self.columns]
        self.rows[...] = (self.old[...].astype(F32) * (1.0 - RATE * DECAY) - RATE * update).astype(BF16)
        self.update[...] = update

    def spread(self, near, far):
        self.first = []
        for side, target in enumerate((near, far)):
            copy = remote(
                self.rows, self.out_weight.at[self.d], self.ag_send.at[side], self.ag_recv.at[side], target
            )
            copy.start()
            self.first.append(copy)
        for i, (src, dst) in enumerate(
            ((self.rows, self.out_weight.at[self.d]), (self.update, self.out_update))
        ):
            copy = pltpu.make_async_copy(src, dst, self.out_sem.at[1 + i])
            copy.start()
            self.outs.append(copy)

    def forward(self, near, far):
        count = self.rows.shape[0]
        cut = count // 2 // 16 * 16
        self.later = []
        for side, (source, target, start, size) in enumerate(
            ((near[0], far, 0, cut), (far[0], near, cut, count - cut))
        ):
            self.first[side].wait_recv()
            if size:
                out = self.out_weight
                spot = out.at[source] if size == count else out.at[source, pl.ds(start, size)]
                copy = remote(spot, spot, self.ag_send.at[2 + side], self.ag_recv.at[2 + side], target)
                copy.start()
                self.later.append(copy)

    def end(self):
        for copy in self.outs + self.later:
            copy.wait()
        for copy in self.first + self.sent:
            copy.wait_send()


def kernel(dp, mp, *refs):
    d, m = lax.axis_index("dp"), lax.axis_index("mp")
    core = lax.rem(m, 2)
    sibling = (d, m + 1 - 2 * core)
    group = [(lax.rem(d + r, dp), m) for r in range(1, dp)]
    line = [(d, lax.rem(m + 2 * r, mp)) for r in range(1, mp // 2)]
    near = (d + 1 - 2 * lax.rem(d, 2), m)
    far = (lax.rem(d + 2, dp), m)
    place = (d, m, core, sibling, group, line)
    scratch = refs[12:]
    count = len(scratch) // 2
    a = Side(place, 0.2 * math.sqrt(D), *refs[0:3], *refs[6:9], scratch[:count])
    b = Side(place, 0.2 * math.sqrt(KEY_VALUE_ROWS), *refs[3:6], *refs[9:12], scratch[count:])
    b.load()
    a.load()
    greet([sibling] + group + line)
    b.scatter()
    b.scatter_sent()
    a.scatter()
    b.local_gram()
    b.core_start()
    b.core_end()
    b.dp_start()
    a.local_gram()
    a.core_start()
    b.dp_end()
    b.line_start()
    a.core_end()
    a.dp_start()
    b.line_end()
    b.line_back()
    a.dp_end()
    a.line_start()
    b.arrived()
    b.dp_back()
    a.line_end()
    a.line_back()
    b.arrived()
    b.core_back()
    a.arrived()
    a.dp_back()
    b.arrived()
    b.unpack()
    b.newton(0)
    a.arrived()
    a.core_back()
    for step in range(1, ITERS):
        b.newton(step)
    b.finish()
    b.spread(near, far)
    a.arrived()
    a.unpack()
    for step in range(ITERS):
        a.newton(step)
    a.finish()
    a.spread(near, far)
    b.forward(near, far)
    a.forward(near, far)
    a.scatter_sent()
    a.end()
    b.end()


def scratch_of(dp, mp, rows, columns):
    zn = mp // 2
    wide = padded(columns)
    total = packed_rows(columns, dp * mp)
    half = total // 2
    quarter = half // dp
    part = quarter // zn
    vmem, sem = pltpu.VMEM, pltpu.SemaphoreType.DMA
    return [
        vmem((rows, columns), BF16),
        vmem((dp - 1, rows, columns), BF16),
        vmem((rows, columns), F32),
        vmem((rows, columns), BF16),
        vmem((rows, columns), F32),
        vmem((rows, columns), F32),
        vmem((rows, columns), BF16),
        vmem((rows, wide), F32),
        vmem((total, BLOCK), F32),
        vmem((half, BLOCK), F32),
        vmem((quarter, BLOCK), F32),
        vmem((part, BLOCK), F32),
        vmem((total, BLOCK), F32),
        vmem((dp - 1, quarter, BLOCK), F32),
        vmem((zn - 1, part, BLOCK), F32),
        vmem((wide, wide), F32),
        vmem((wide, wide), F32),
        vmem((wide, wide), F32),
        vmem((wide, 3 * wide), BF16),
        vmem((3 * wide, wide), BF16),
        sem((3,)),
        sem((3,)),
        sem((dp - 1,)),
        sem((dp - 1,)),
        sem((4,)),
        sem((4, dp - 1)),
        sem((4, zn - 1)),
        sem((4,)),
        sem((4,)),
    ]


def local(dp, mp, *args):
    (ra, ca), (rb, cb) = args[1].shape, args[4].shape
    hbm = pl.BlockSpec(memory_space=pl.ANY)
    shape = jax.ShapeDtypeStruct
    return pl.pallas_call(
        functools.partial(kernel, dp, mp),
        out_shape=[
            shape((dp, ra, ca), BF16), shape((ra, ca), F32), shape((ra, ca), F32),
            shape((dp, rb, cb), BF16), shape((rb, cb), F32), shape((rb, cb), F32),
        ],
        in_specs=[hbm] * 6,
        out_specs=[hbm] * 6,
        scratch_shapes=scratch_of(dp, mp, ra, ca) + scratch_of(dp, mp, rb, cb),
        compiler_params=pltpu.CompilerParams(
            collective_id=0, has_side_effects=True, vmem_limit_bytes=56 * 2**20
        ),
    )(*args)


def solution(mesh):
    both = P(("dp", "mp"), None)
    grads = P("dp", None, "mp", None)
    weights = P(None, "mp", None)
    return jax.shard_map(
        functools.partial(local, mesh.shape["dp"], mesh.shape["mp"]),
        mesh=mesh,
        in_specs=(grads, both, both, grads, both, both),
        out_specs=(weights, both, both, weights, both, both),
        check_vma=False,
    )
```

time: 632 us -> 115 us (0.18)
  waiting for transfers between devices: 491 us -> 0 us
  Pallas kernels: 0 us -> 105 us
  blocking collectives: 56.3 us -> 0 us
  matrix products: 55.5 us -> 0 us
  between operations: 16.1 us -> 0.67 us
    psum x3 -> x0, waiting for transfers between devices: 407 us -> none  [local(): lax.psum((gram_of(iterates[0]), gram_of(iterates[1])), ('dp', 'mp'))]
    pallas_call x0 -> x1, Pallas kernels: none -> 105 us  [local(): pl.pallas_call(functools.partial(kernel, dp, mp), out_shape=[shape((dp, r...]
    unnamed x8 -> x0, waiting for transfers between devices: 69.8 us -> none
    dot_general x18 -> x0, matrix products: 55.5 us -> none  [the longest x6 24.4 us: newton(): jnp.dot(gram_matrix, gram_matrix, precision=PRECISE, preferred_element_ty...]
    psum x1 -> x0, blocking collectives: 39 us -> none  [local(): lax.psum((jnp.sum(directions[0] * directions[0]), jnp.sum(directions[1] *...]
    all_gather x1 -> x0, blocking collectives: 17.3 us -> none  [local(): lax.all_gather(new_rows[0][None], 'dp', axis=0, tiled=True)]
    all_gather x1 -> x0, waiting for transfers between devices: 14.8 us -> none  [local(): lax.all_gather(new_rows[1][None], 'dp', axis=0, tiled=True)]
  transfers between devices with their start and end apart: 6 -> 0, of which waited for: 6 -> 0; matrix products, arithmetic and copies ran while one was open for 2% -> 0% of each run, Pallas kernels for 0% -> 0%
where the time goes in v2:
time: 115 us
  Pallas kernels  105 us (91%)
  local copies, waits for them, and re-layouts  8.67 us (8%)
    pallas_call x1, Pallas kernels, local(): pl.pallas_call(functools.partial(kernel, dp, mp), out_shape=[shape((dp, r...  105 us
    unnamed x16, local copies, waits for them, and re-layouts  8.67 us

profile of v2, /device:TPU:1, one launch (start us, length us, event | category | flops | bytes accessed | tf_op | source)
XLA Modules:
  0.0 114.8 jit_solution(5030123742283958419)
XLA Ops:
  0.6 105.5 %shard_map.109 = (bf16[4,224,576]{2,1,0:T(8,128)(2,1)}, f32[224,576]{1,0:T(8,128)}, f32[224,576]{1,0:T(8,128)}, bf16[4,512,512]{2,1,0:T(8,128)(2,1)}, f32[512,512]{1,0:T(8,128)}, /*index=5*/f32[512,512]{1,0:T(8,128)}) custom-call(bf16[1,4,224,576]{3,2,1,0:T(8,128)(2,1)} %refs_0_.1, f32[224,576]{1,0:T(8,128)} %refs_1_.1, bf16[224,576]{1,0:T(8,128)(2,1)} %refs_2_.1, ...), custom_call_target="tpu_custom_call" | custom-call | tf_op jit(solution)/shard_map/pallas_call | solution.py:429
  106.1 0.0 copy-start.4
  106.1 0.0 copy-start.3
  106.1 0.0 copy-start
  106.1 2.5 %copy.18 = bf16[4,224,576]{2,1,0:T(8,128)(2,1)} copy(bf16[4,224,576]{2,1,0:T(8,128)(2,1)} %get-tuple-element.12) | data formatting | bytes 2064384
  108.6 0.0 copy-done.4
  108.6 0.8 copy.19
  109.5 0.0 copy-done.3
  109.5 0.8 copy.20
  110.3 0.0 copy-done
  110.3 0.0 copy-start.2
  110.3 1.3 %copy.21 = bf16[4,512,512]{2,1,0:T(8,128)(2,1)} copy(bf16[4,512,512]{2,1,0:T(8,128)(2,1)S(1)} %copy-done) | data formatting | bytes 4194304
  111.6 0.6 copy-done.2
  112.2 0.0 copy-start.1
  112.2 1.0 copy.22
  113.2 0.6 copy-done.1
  113.8 1.0 copy.23
Async XLA Ops:
  106.1 2.5 %copy-start.4 = (f32[224,576]{1,0:T(8,128)S(1)}, f32[224,576]{1,0:T(8,128)}, u32[]{:S(2)}) copy-start(f32[224,576]{1,0:T(8,128)} %get-tuple-element.13) | copy-start | bytes 1548292
  106.1 3.3 %copy-start.3 = (f32[224,576]{1,0:T(8,128)S(1)}, f32[224,576]{1,0:T(8,128)}, u32[]{:S(2)}) copy-start(f32[224,576]{1,0:T(8,128)} %get-tuple-element.14) | copy-start | bytes 1548292
  106.1 4.1 %copy-start = (bf16[4,512,512]{2,1,0:T(8,128)(2,1)S(1)}, bf16[4,512,512]{2,1,0:T(8,128)(2,1)}, u32[]{:S(2)}) copy-start(bf16[4,512,512]{2,1,0:T(8,128)(2,1)} %get-tuple-element.15) | copy-start | bytes 6291460
  110.3 2.0 %copy-start.2 = (f32[512,512]{1,0:T(8,128)S(1)}, f32[512,512]{1,0:T(8,128)}, u32[]{:S(2)}) copy-start(f32[512,512]{1,0:T(8,128)} %get-tuple-element.16) | copy-start | bytes 3145732
  112.2 1.6 %copy-start.1 = (f32[512,512]{1,0:T(8,128)S(1)}, f32[512,512]{1,0:T(8,128)}, u32[]{:S(2)}) copy-start(f32[512,512]{1,0:T(8,128)} %get-tuple-element.17) | copy-start | bytes 3145732

commit v3 on v2

--- a/solution.py
+++ b/solution.py
@@ -62,19 +62,23 @@
     return pl.ds(pl.multiple_of(start, 8), size)
 
 
+def part_of(ref, start, size):
+    return ref if size == ref.shape[-2] else ref.at[pl.ds(start, size)]
+
+
 class Side:
     def __init__(self, place, gain, grads, mom_in, old_in, out_weight, out_state, out_update, scratch):
         self.place, self.gain = place, gain
         self.grads, self.mom_in, self.old_in = grads, mom_in, old_in
         self.out_weight, self.out_state, self.out_update = out_weight, out_state, out_update
         (
-            self.own, self.got, self.mom, self.old, self.state, self.update, self.rows, self.iterate,
+            self.own, self.pair_own, self.pair_got, self.pair_sum, self.last_got, self.mom, self.old, self.state, self.update, self.rows, self.iterate,
             self.pack, self.half, self.quarter, self.part, self.red, self.quart_recv, self.part_recv,
             self.gram, self.poly, self.inner, self.left, self.right,
             self.in_sem, self.out_sem, self.rs_send, self.rs_recv, self.core_sem,
             self.dp_sem, self.line_sem, self.ag_send, self.ag_recv,
         ) = scratch
-        self.d, self.m, self.core, self.sibling, self.group, self.line = place
+        self.d, self.m, self.core, self.sibling, self.group, self.line, near, far, across = place
         self.columns = self.mom.shape[1]
         self.wide = self.iterate.shape[1]
         self.z = self.m // 2
@@ -86,28 +90,60 @@
         self.my_quarter = self.my_half + self.d * self.quarter_rows
         self.my_part = self.my_quarter + self.z * self.part_rows
         self.sent = []
+        count = self.own.shape[0]
+        cut = count // 2 // 16 * 16
+        self.ways = [
+            (way, start, size, first, second)
+            for way, (start, size, first, second) in enumerate(
+                ((0, cut, near, far), (cut, count - cut, far, near))
+            )
+            if size
+        ]
+        self.across = across
 
     def load(self):
         self.loads = []
-        for i, (src, dst) in enumerate(
-            ((self.grads.at[0, self.d], self.own), (self.mom_in, self.mom), (self.old_in, self.old))
-        ):
+        pairs = [(self.grads.at[0, self.d], self.own), (self.mom_in, self.mom), (self.old_in, self.old)]
+        for way, start, size, first, second in self.ways:
+            pairs.append(
+                (part_of(self.grads.at[0, second[0]], start, size), part_of(self.pair_own, start, size))
+            )
+        for i, (src, dst) in enumerate(pairs):
             copy = pltpu.make_async_copy(src, dst, self.in_sem.at[i])
             copy.start()
             self.loads.append(copy)
 
     def scatter(self):
-        self.scattered = []
-        for r, target in enumerate(self.group):
+        self.scattered = {}
+        for kind in range(2):
+            for way, start, size, first, second in self.ways:
+                owner = self.across if kind == 0 else first[0]
+                copy = remote(
+                    part_of(self.grads.at[0, owner], start, size), part_of(self.pair_got.at[kind], start, size),
+                    self.rs_send.at[kind, way], self.rs_recv.at[kind, way], first,
+                )
+                copy.start()
+                self.scattered[kind, way] = copy
+
+    def scatter_sent(self):
+        for copy in self.scattered.values():
+            copy.wait_send()
+
+    def scatter_pairs(self):
+        for i in range(len(self.ways)):
+            self.loads[3 + i].wait()
+        for way, start, size, first, second in self.ways:
+            self.scattered[0, way].wait_recv()
+            rows = slice(start, start + size)
+            self.pair_sum[rows] = (
+                self.pair_own[rows].astype(F32) + self.pair_got[0, rows].astype(F32)
+            ).astype(BF16)
             copy = remote(
-                self.grads.at[0, target[0]], self.got.at[r], self.rs_send.at[r], self.rs_recv.at[r], target
+                part_of(self.pair_sum, start, size), part_of(self.last_got, start, size),
+                self.rs_send.at[2, way], self.rs_recv.at[2, way], second,
             )
             copy.start()
-            self.scattered.append(copy)
-
-    def scatter_sent(self):
-        for copy in self.scattered:
-            copy.wait_send()
+            self.scattered[2, way] = copy
 
     def local_gram(self):
         used = len(block_list(self.columns)) * BLOCK
@@ -118,13 +154,14 @@
         for ref in (self.gram, self.poly, self.inner):
             if self.wide > self.columns:
                 ref[...] = jnp.zeros(ref.shape, F32)
-        for copy in self.loads:
+        for copy in self.loads[:3]:
             copy.wait()
-        for copy in self.scattered:
-            copy.wait_recv()
-        summed = self.own[...].astype(F32)
-        for r in range(len(self.group)):
-            summed = summed + self.got[r].astype(F32)
+        for kind in (1, 2):
+            for way, *_ in self.ways:
+                self.scattered[kind, way].wait_recv()
+        summed = (
+            self.own[...].astype(F32) + self.pair_got[1].astype(F32) + self.last_got[...].astype(F32)
+        )
         state = MOMENT * self.mom[...] + summed
         self.state[...] = state
         self.iterate[:, : self.columns] = summed + MOMENT * state
@@ -326,7 +363,8 @@
     line = [(d, lax.rem(m + 2 * r, mp)) for r in range(1, mp // 2)]
     near = (d + 1 - 2 * lax.rem(d, 2), m)
     far = (lax.rem(d + 2, dp), m)
-    place = (d, m, core, sibling, group, line)
+    across = near[0] + 2 - 4 * (d // 2)
+    place = (d, m, core, sibling, group, line, near, far, across)
     scratch = refs[12:]
     count = len(scratch) // 2
     a = Side(place, 0.2 * math.sqrt(D), *refs[0:3], *refs[6:9], scratch[:count])
@@ -337,6 +375,9 @@
     b.scatter()
     b.scatter_sent()
     a.scatter()
+    b.scatter_pairs()
+    a.scatter_sent()
+    a.scatter_pairs()
     b.local_gram()
     b.core_start()
     b.core_end()
@@ -376,7 +417,9 @@
     a.spread(near, far)
     b.forward(near, far)
     a.forward(near, far)
-    a.scatter_sent()
+    for side in (a, b):
+        for way, *_ in side.ways:
+            side.scattered[2, way].wait_send()
     a.end()
     b.end()
 
@@ -391,7 +434,10 @@
     vmem, sem = pltpu.VMEM, pltpu.SemaphoreType.DMA
     return [
         vmem((rows, columns), BF16),
-        vmem((dp - 1, rows, columns), BF16),
+        vmem((rows, columns), BF16),
+        vmem((2, rows, columns), BF16),
+        vmem((rows, columns), BF16),
+        vmem((rows, columns), BF16),
         vmem((rows, columns), F32),
         vmem((rows, columns), BF16),
         vmem((rows, columns), F32),
@@ -410,10 +456,10 @@
         vmem((wide, wide), F32),
         vmem((wide, 3 * wide), BF16),
         vmem((3 * wide, wide), BF16),
+        sem((5,)),
         sem((3,)),
-        sem((3,)),
-        sem((dp - 1,)),
-        sem((dp - 1,)),
+        sem((3, 2)),
+        sem((3, 2)),
         sem((4,)),
         sem((4, dp - 1)),
         sem((4, zn - 1)),
@@ -426,7 +472,7 @@
     (ra, ca), (rb, cb) = args[1].shape, args[4].shape
     hbm = pl.BlockSpec(memory_space=pl.ANY)
     shape = jax.ShapeDtypeStruct
-    return pl.pallas_call(
+    results = pl.pallas_call(
         functools.partial(kernel, dp, mp),
         out_shape=[
             shape((dp, ra, ca), BF16), shape((ra, ca), F32), shape((ra, ca), F32),
@@ -439,6 +485,39 @@
             collective_id=0, has_side_effects=True, vmem_limit_bytes=56 * 2**20
         ),
     )(*args)
+    return place_results(results)
+
+
+def place_kernel(count, *refs):
+    sem = refs[-1]
+    copies = []
+    for src, dst in zip(refs[:count], refs[count : 2 * count]):
+        rows = src.shape[-2]
+        if len(src.shape) == 3:
+            views = [(k,) for k in range(src.shape[0])]
+        else:
+            pieces = 4 if rows % 64 == 0 else 2 if rows % 32 == 0 else 1
+            size = rows // pieces
+            views = [(pl.ds(k * size, size),) for k in range(pieces)]
+        for view in views:
+            copies.append(pltpu.make_async_copy(src.at[view], dst.at[view], sem.at[len(copies)]))
+    for copy in copies:
+        copy.start()
+    for copy in copies:
+        copy.wait()
+
+
+def place_results(results):
+    count = len(results)
+    hbm = pl.BlockSpec(memory_space=pl.ANY)
+    return pl.pallas_call(
+        functools.partial(place_kernel, count),
+        out_shape=[jax.ShapeDtypeStruct(r.shape, r.dtype) for r in results],
+        in_specs=[hbm] * count,
+        out_specs=[hbm] * count,
+        scratch_shapes=[pltpu.SemaphoreType.DMA((4 * count,))],
+        compiler_params=pltpu.CompilerParams(vmem_limit_bytes=56 * 2**20),
+    )(*results)
 
 
 def solution(mesh):

time: 115 us -> 297 us (2.58)
  Pallas kernels: 105 us -> 296 us
  local copies, waits for them, and re-layouts: 8.67 us -> 0 us
    pallas_call x0 -> x1, Pallas kernels: none -> 198 us  [place_results(): pl.pallas_call(functools.partial(place_kernel, count), out_shape=[jax.Sha...]
    unnamed x16 -> x0, local copies, waits for them, and re-layouts: 8.67 us -> none
    pallas_call x1, Pallas kernels: 105 us -> 98 us  [local(): pl.pallas_call(functools.partial(kernel, dp, mp), out_shape=[shape((dp, r...]
where the time goes in v3:
time: 297 us
  Pallas kernels  296 us (100%)
    pallas_call x1, Pallas kernels, place_results(): pl.pallas_call(functools.partial(place_kernel, count), out_shape=[jax.Sha...  198 us
    pallas_call x1, Pallas kernels, local(): pl.pallas_call(functools.partial(kernel, dp, mp), out_shape=[shape((dp, r...  98 us

profile of v3, /device:TPU:1, one launch (start us, length us, event | category | flops | bytes accessed | tf_op | source)
XLA Modules:
  0.0 296.6 jit_solution(10508984584176553027)
XLA Ops:
  0.6 98.0 %shard_map.109 = (bf16[4,224,576]{2,1,0:T(8,128)(2,1)}, f32[224,576]{1,0:T(8,128)}, f32[224,576]{1,0:T(8,128)}, bf16[4,512,512]{2,1,0:T(8,128)(2,1)}, f32[512,512]{1,0:T(8,128)}, /*index=5*/f32[512,512]{1,0:T(8,128)}) custom-call(bf16[1,4,224,576]{3,2,1,0:T(8,128)(2,1)} %refs_0_.1, f32[224,576]{1,0:T(8,128)} %refs_1_.1, bf16[224,576]{1,0:T(8,128)(2,1)} %refs_2_.1, ...), custom_call_target="tpu_custom_call" | custom-call | tf_op jit(solution)/shard_map/pallas_call | solution.py:475
  98.6 197.9 %shard_map.110 = (bf16[4,224,576]{2,1,0:T(8,128)(2,1)}, f32[224,576]{1,0:T(8,128)}, f32[224,576]{1,0:T(8,128)}, bf16[4,512,512]{2,1,0:T(8,128)(2,1)}, f32[512,512]{1,0:T(8,128)}, /*index=5*/f32[512,512]{1,0:T(8,128)}) custom-call(bf16[4,224,576]{2,1,0:T(8,128)(2,1)} %get-tuple-element.12.refs_0_, f32[224,576]{1,0:T(8,128)} %get-tuple-element.13.refs_1_, ...), custom_call_target="tpu_custom_call" | custom-call | tf_op jit(solution)/shard_map/pallas_call | solution.py:513

commit v4 on v3

--- a/solution.py
+++ b/solution.py
@@ -490,8 +490,8 @@
 
 def place_kernel(count, *refs):
     sem = refs[-1]
-    copies = []
-    for src, dst in zip(refs[:count], refs[count : 2 * count]):
+    loads, stores = [], []
+    for src, dst, stage in zip(refs[:count], refs[count : 2 * count], refs[2 * count : 3 * count]):
         rows = src.shape[-2]
         if len(src.shape) == 3:
             views = [(k,) for k in range(src.shape[0])]
@@ -500,11 +500,16 @@
             size = rows // pieces
             views = [(pl.ds(k * size, size),) for k in range(pieces)]
         for view in views:
-            copies.append(pltpu.make_async_copy(src.at[view], dst.at[view], sem.at[len(copies)]))
-    for copy in copies:
-        copy.start()
-    for copy in copies:
-        copy.wait()
+            k = len(loads)
+            loads.append(pltpu.make_async_copy(src.at[view], stage.at[view], sem.at[0, k]))
+            stores.append(pltpu.make_async_copy(stage.at[view], dst.at[view], sem.at[1, k]))
+    for load in loads:
+        load.start()
+    for load, store in zip(loads, stores):
+        load.wait()
+        store.start()
+    for store in stores:
+        store.wait()
 
 
 def place_results(results):
@@ -515,7 +520,8 @@
         out_shape=[jax.ShapeDtypeStruct(r.shape, r.dtype) for r in results],
         in_specs=[hbm] * count,
         out_specs=[hbm] * count,
-        scratch_shapes=[pltpu.SemaphoreType.DMA((4 * count,))],
+        scratch_shapes=[pltpu.VMEM(r.shape, r.dtype) for r in results]
+        + [pltpu.SemaphoreType.DMA((2, 4 * count))],
         compiler_params=pltpu.CompilerParams(vmem_limit_bytes=56 * 2**20),
     )(*results)
 

time: 297 us -> 105 us (0.35)
  Pallas kernels: 296 us -> 104 us
    pallas_call x1, Pallas kernels: 198 us -> 5.62 us  [place_results(): pl.pallas_call(functools.partial(place_kernel, count), out_shape=[jax.Sha...]
where the time goes in v4:
time: 105 us; the launch traced here: 104 us
  Pallas kernels  104 us (99%)
    pallas_call x1, Pallas kernels, local(): pl.pallas_call(functools.partial(kernel, dp, mp), out_shape=[shape((dp, r...  98 us
    pallas_call x1, Pallas kernels, place_results(): pl.pallas_call(functools.partial(place_kernel, count), out_shape=[jax.Sha...  5.62 us

profile of v4, /device:TPU:1, one launch (start us, length us, event | category | flops | bytes accessed | tf_op | source)
XLA Modules:
  0.0 104.4 jit_solution(9910244801055992318)
XLA Ops:
  0.6 98.0 %shard_map.109 = (bf16[4,224,576]{2,1,0:T(8,128)(2,1)}, f32[224,576]{1,0:T(8,128)}, f32[224,576]{1,0:T(8,128)}, bf16[4,512,512]{2,1,0:T(8,128)(2,1)}, f32[512,512]{1,0:T(8,128)}, /*index=5*/f32[512,512]{1,0:T(8,128)}) custom-call(bf16[1,4,224,576]{3,2,1,0:T(8,128)(2,1)} %refs_0_.1, f32[224,576]{1,0:T(8,128)} %refs_1_.1, bf16[224,576]{1,0:T(8,128)(2,1)} %refs_2_.1, ...), custom_call_target="tpu_custom_call" | custom-call | tf_op jit(solution)/shard_map/pallas_call | solution.py:475
  98.6 5.6 %shard_map.110 = (bf16[4,224,576]{2,1,0:T(8,128)(2,1)}, f32[224,576]{1,0:T(8,128)}, f32[224,576]{1,0:T(8,128)}, bf16[4,512,512]{2,1,0:T(8,128)(2,1)}, f32[512,512]{1,0:T(8,128)}, /*index=5*/f32[512,512]{1,0:T(8,128)}) custom-call(bf16[4,224,576]{2,1,0:T(8,128)(2,1)} %get-tuple-element.12.refs_0_, f32[224,576]{1,0:T(8,128)} %get-tuple-element.13.refs_1_, ...), custom_call_target="tpu_custom_call" | custom-call | tf_op jit(solution)/shard_map/pallas_call | solution.py:518
